TPU v7x, 128 devices: a whole 4x4x4 slice. The times are simulated.
128 devices in a mesh: seq: 8 (over x_hi, z), doc: 16 (over x_lo, y, core).
Axes of the slice: x: 4 (x_hi: 2, x_lo: 2; x = x_hi * 2 + x_lo), y: 4, z: 4, core: 2. Of those that a mesh axis runs over, the one named last changes fastest.
Arguments:
- hidden_in: bfloat16 [16, 1024, 2880], P('doc', 'seq'), may hold values from -6 to 6
- queries: bfloat16 [16, 1024, 4096], P('doc', 'seq'), may hold values from -8 to 8
- key_heads: bfloat16 [16, 1024, 512], P('doc', 'seq'), may hold values from -8 to 8
- values: bfloat16 [16, 1024, 512], P('doc', 'seq'), may hold values from -6 to 6
- doc_lengths: int32 [16], P('doc'), may hold values from 1 to 1024, 10240 in all
- out_weight: bfloat16 [4096, 2880], P('seq'), may hold values from -0.75 to 0.75
- norm_gain: bfloat16 [2880], replicated, may hold values from 0.099609375 to 1.8984375
- router_weight: bfloat16 [2880, 64], replicated, may hold values from -0.109375 to 0.109375
- expert_ids: int32 [16, 1024, 4], P('doc', 'seq'), may hold values from 0 to 63, all different within a row; in each aligned block of 128 rows (0 to 127, 128 to 255, ..., all dimensions but the last counted through in order) at most 12 rows name the same one
- gate_weight: bfloat16 [128, 2880, 768], P(('seq', 'doc')), may hold values from -0.109375 to 0.109375
- up_weight: bfloat16 [128, 2880, 768], P(('seq', 'doc')), may hold values from -0.109375 to 0.109375
- down_weight: bfloat16 [128, 768, 2880], P(('seq', 'doc')), may hold values from -0.15625 to 0.15625
Outputs:
- layer_out: bfloat16 [16, 1024, 2880], P('doc', 'seq')
Inputs may be any that keep to these rules, and one draw needn't show every extreme that they name: `doc_lengths`: the lengths sum to 10240, and the longest is 1024. `expert_ids`: each token names 4 different experts. Among the 128 positions that one device holds (aligned blocks of a document), no expert is named more than 12 times, and in some such block an expert is named exactly 12 times.
All inputs are finite; a program needn't handle non-finite values. No bound on the sum of `doc_lengths` on one device may be relied on, other than what follows from the above.
Results may differ from a plain program's by a relative error of at most 0.02.
Values may be sent and summed in bfloat16 or wider, within the bound.
No kernel may reach another device: no remote copies, remote signals or barrier semaphores. Data moves between devices by JAX's collectives and lax.ppermute only.
A program may use at most 128 MiB of HBM per device.

v0:
```python
import jax
import jax.numpy as jnp
from jax import lax
from jax.sharding import PartitionSpec as P

HEADS = 64
KVH = 8
HD = 64
TOP = 4


negative_fill = -1e30
swiglu_alpha = 1.702
norm_eps = 1e-05


def rounded(tensor_in):
    return lax.optimization_barrier(tensor_in.astype(jnp.bfloat16))


def local(
    hidden_in,
    queries,
    key_heads,
    values,
    doc_lengths,
    out_weight,
    norm_gain,
    router_weight,
    expert_ids,
    gate_weight,
    up_weight,
    down_weight,
):
    tokens_dev = hidden_in.shape[1]
    model_width = hidden_in.shape[2]
    doc_length = doc_lengths[0]
    group_size = HEADS // KVH
    score_scale = HD ** (-0.5)
    own_queries = queries[0].reshape(tokens_dev, KVH, group_size, HD)
    query_pos = lax.axis_index("seq") * tokens_dev + jnp.arange(tokens_dev, dtype=jnp.int32)
    run_top = jnp.full((KVH, group_size, tokens_dev), negative_fill, jnp.float32)
    piece_keys = lax.all_gather(key_heads, "seq", axis=1, tiled=True)
    piece_values = lax.all_gather(values, "seq", axis=1, tiled=True)
    piece_rows = piece_keys.shape[1]
    key_block = piece_keys[0].reshape(piece_rows, KVH, HD)
    value_block = piece_values[0].reshape(piece_rows, KVH, HD)
    key_pos = jnp.arange(piece_rows, dtype=jnp.int32)
    allowed = (key_pos[None, :] <= query_pos[:, None]) & (key_pos[None, :] < doc_length)
    scores = (
        jnp.einsum("qkgd,jkd->kgqj", own_queries, key_block, preferred_element_type=jnp.float32)
        * score_scale
    )
    scores = jnp.where(allowed, scores, negative_fill)
    new_top = jnp.maximum(run_top, jnp.max(scores, axis=-1))
    weights = jnp.where(allowed, jnp.exp(scores - new_top[..., None]), 0.0)
    new_total = jnp.sum(weights, axis=-1)
    update = jnp.einsum(
        "kgqj,jkd->kgqd",
        weights.astype(jnp.bfloat16),
        value_block,
        preferred_element_type=jnp.float32,
    )
    own_out = (update / new_total[..., None]).astype(jnp.bfloat16)
    own_out = own_out.transpose(2, 0, 1, 3).reshape(1, tokens_dev, HEADS * HD)
    attended = lax.all_to_all(own_out, "seq", split_axis=2, concat_axis=1, tiled=True)[0]
    attention_sum = lax.psum_scatter(
        jnp.dot(attended, out_weight, preferred_element_type=jnp.float32).astype(jnp.bfloat16),
        "seq",
        scatter_dimension=0,
        tiled=True,
    ).astype(jnp.float32)
    residual = rounded(hidden_in[0].astype(jnp.float32) + attention_sum).astype(jnp.float32)
    mean_square = jnp.mean(residual * residual, axis=-1, keepdims=True)
    normed = (residual * lax.rsqrt(mean_square + norm_eps) * norm_gain.astype(jnp.float32)).astype(
        jnp.bfloat16
    )
    logits = jnp.dot(normed, router_weight, preferred_element_type=jnp.float32)
    expert_count = router_weight.shape[1]
    chosen_ids = expert_ids[0]
    expert_range = jnp.arange(expert_count, dtype=jnp.int32)
    matches = chosen_ids[:, :, None] == expert_range[None, None, :]
    chosen_logits = jnp.sum(jnp.where(matches, logits[:, None, :], 0.0), axis=-1)
    raised = jnp.exp(chosen_logits)
    route_share = raised / jnp.sum(raised, axis=-1, keepdims=True)
    capacity = 2 * (tokens_dev * TOP * 3 // (4 * expert_count))
    flat_ids = chosen_ids.reshape(-1)
    one_hot = (flat_ids[:, None] == expert_range[None, :]).astype(jnp.int32)
    slot_rank = jnp.sum(jnp.cumsum(one_hot, axis=0) * one_hot, axis=1) - 1
    dest_row = flat_ids * capacity + slot_rank
    pair_count = tokens_dev * TOP
    slot_table = (
        jnp.full((expert_count * capacity,), tokens_dev, jnp.int32)
        .at[dest_row]
        .set(jnp.arange(pair_count, dtype=jnp.int32) // TOP)
    )
    padded = jnp.concatenate([normed, jnp.zeros((1, model_width), jnp.bfloat16)], axis=0)
    outgoing = padded[slot_table].reshape(expert_count, capacity, model_width)
    doubled = jnp.broadcast_to(outgoing[:, None], (expert_count, 2, capacity, model_width)).reshape(
        2 * expert_count, capacity, model_width
    )
    arrived = lax.all_to_all(doubled, ("seq", "doc"), split_axis=0, concat_axis=0, tiled=True)
    flat_rows = arrived.reshape(-1, model_width)
    gate_val = jnp.dot(flat_rows, gate_weight[0], preferred_element_type=jnp.float32)
    up_val = jnp.dot(flat_rows, up_weight[0], preferred_element_type=jnp.float32)
    active = (gate_val * jax.nn.sigmoid(swiglu_alpha * gate_val) * (up_val + 1.0)).astype(
        jnp.bfloat16
    )
    arrived_back = lax.all_to_all(
        jnp.dot(active, down_weight[0], preferred_element_type=jnp.float32)
        .astype(jnp.bfloat16)
        .reshape(arrived.shape),
        ("seq", "doc"),
        split_axis=0,
        concat_axis=0,
        tiled=True,
    )
    arrived_back = arrived_back.reshape(expert_count, 2, capacity, model_width)
    expert_out = rounded(
        arrived_back[:, 0].astype(jnp.float32) + arrived_back[:, 1].astype(jnp.float32)
    )
    expert_out = expert_out.reshape(expert_count * capacity, model_width)
    gathered = expert_out[dest_row].reshape(tokens_dev, TOP, model_width)
    mixture_sum = jnp.einsum("tk,tkd->td", route_share, gathered.astype(jnp.float32))
    layer_out = (residual + mixture_sum).astype(jnp.bfloat16)
    return layer_out[None]


def solution(mesh):
    in_specs = (
        P("doc", "seq", None),
        P("doc", "seq", None),
        P("doc", "seq", None),
        P("doc", "seq", None),
        P("doc"),
        P("seq", None),
        P(),
        P(),
        P("doc", "seq", None),
        P(("seq", "doc"), None, None),
        P(("seq", "doc"), None, None),
        P(("seq", "doc"), None, None),
    )
    out_specs = P("doc", "seq", None)
    return jax.shard_map(local, mesh=mesh, in_specs=in_specs, out_specs=out_specs, check_vma=False)
```

profile of v0, /device:TPU:32, one launch (start us, length us, event | category | flops | bytes accessed | tf_op | source)
XLA Modules:
  0.0 778.6 jit_solution(9515316538338982292)
XLA Ops:
  11.2 46.7 %all-gather.3.cloned.1.call-done = bf16[1,1024,512]{2,1,0:T(8,128)(2,1)} async-done(((bf16[1,128,512]{2,1,0:T(8,128)(2,1)}), bf16[1,1024,512]{2,1,0:T(8,128)(2,1)}) %all-gather.3.cloned.1.call-update) | async-done | bytes 1048592 | tf_op jit(solution)/shard_map/all_gather | solution.py:43
  60.1 14.7 %fusion = (f32[8,8,128]{2,1,0:T(8,128)S(1)}, f32[8,1024,128,8]{2,1,3,0:T(8,128)}) fusion(pred[128,1024]{0,1:T(8,128)(4,1)S(1)} %fusion.27, bf16[1024,8,64,1]{0,2,3,1:T(8,128)(2,1)} %bitcast.110, bf16[128,8,8,64]{0,3,2,1:T(8,128)(2,1)} %bitcast.109), kind=kOutput, calls=%fused_computation.5 | convolution fusion | flops 1098899456 | bytes 35815424 | tf_op jit(solution)/shard_map/qkgd,jkd->kgqj/dot_general | solution.py:51
  74.8 14.9 %fusion.1 = f32[8,8,128]{2,1,0:T(8,128)S(1)} fusion(f32[8,1024,128,8]{2,1,3,0:T(8,128)} %get-tuple-element.6, f32[8,8,128]{2,1,0:T(8,128)S(1)} %broadcast_maximum_fusion, pred[128,1024]{0,1:T(8,128)(4,1)S(1)} %fusion.27), kind=kLoop, calls=%fused_computation.6 | loop fusion | flops 41934848 | bytes 33751040 | tf_op jit(solution)/shard_map/reduce_sum | solution.py:57
  89.7 15.7 %all-gather.5.cloned.1.call-done = bf16[1,1024,512]{2,1,0:T(8,128)(2,1)} async-done(((bf16[1,128,512]{2,1,0:T(8,128)(2,1)}), bf16[1,1024,512]{2,1,0:T(8,128)(2,1)}) %all-gather.5.cloned.1.call-update) | async-done | bytes 1048592 | tf_op jit(solution)/shard_map/all_gather | solution.py:44
  107.7 14.5 %fusion.18 = bf16[128,8,8,64]{0,3,2,1:T(8,128)(2,1)S(1)} fusion(bf16[1024,8,64,1]{0,2,3,1:T(8,128)(2,1)} %bitcast.113, f32[8,1024,128,8]{2,1,3,0:T(8,128)} %get-tuple-element.6, f32[8,8,128]{2,1,0:T(8,128)S(1)} %broadcast_maximum_fusion, pred[128,1024]{0,1:T(8,128)(4,1)S(1)} %fusion.27, f32[128,8,8]{0,2,1:T(8,128)S(1)} %bitcast.115), kind=kOutput, calls=%fused_computation.28 | convolution fusion | flops 1116733440 | bytes 35848192 | tf_op jit(solution)/shard_map/kgqj,jkd->kgqd/dot_general | solution.py:58
  122.2 17.2 %copy.101 = bf16[1,128,4096]{1,0,2:T(2,128)(2,1)} copy(bf16[1,128,4096]{1,2,0:T(8,128)(2,1)S(1)} %bitcast.112) | data formatting | bytes 2097152 | tf_op jit(solution)/shard_map/reshape | solution.py:65
  140.0 24.4 %reduce.2 = bf16[4096,128]{1,0:T(8,128)(2,1)} reduce(bf16[4096,1,128]{2,1,0:T(2,128)(2,1)} %bitcast.108, bf16[]{:T(256)} %broadcast.127), dimensions={1}, to_apply=%bitcast.104.reduce_sub_computation | reduce | bytes 2097154
  166.5 19.6 %all_to_all.25 = bf16[8,2,32768]{2,1,0:T(2,128)(2,1)} all-to-all(bf16[8,2,32768]{2,1,0:T(2,128)(2,1)} %reshape.147), channel_id=1, replica_groups=mesh['seq'=8,'doc'=16] {'seq'}, dimensions={0} | all-to-all | bytes 2097152 | tf_op jit(solution)/shard_map/all_to_all | solution.py:66
  196.9 6.3 convolution_convert_fusion.1
  203.2 8.5 %copy.90 = bf16[1024,2880]{1,0:T(8,128)(2,1)} copy(bf16[1024,2880]{0,1:T(8,128)(2,1)} %convolution_convert_fusion.1) | data formatting | bytes 11796480
  217.6 88.7 %reduce-scatter.4.cloned.1.call-done = bf16[128,2880]{1,0:T(8,128)(2,1)} async-done(((bf16[1024,2880]{1,0:T(8,128)(2,1)}), bf16[128,2880]{1,0:T(8,128)(2,1)}) %reduce-scatter.4.cloned.1.call-update) | async-done | bytes 737296 | tf_op jit(solution)/shard_map/reduce_scatter | solution.py:67
  313.7 7.3 broadcast_in_dim.65
  325.5 143.4 %all_to_all.26 = bf16[128,12,2880]{2,1,0:T(8,128)(2,1)} all-to-all(bf16[128,12,2880]{2,1,0:T(8,128)(2,1)S(1)} %bitcast.106), channel_id=1, replica_groups=mesh['seq'=8,'doc'=16] {'seq','doc'}, dimensions={0} | all-to-all | bytes 17694720 | tf_op jit(solution)/shard_map/all_to_all | solution.py:102
  468.9 14.6 %reshape.107 = bf16[1536,2880]{1,0:T(8,128)(2,1)} reshape(bf16[128,12,2880]{2,1,0:T(8,128)(2,1)} %all_to_all.26) | data formatting | bytes 17694720 | tf_op jit(solution)/shard_map/reshape | solution.py:103
  483.5 12.7 %fusion.8 = f32[1536,768]{1,0:T(8,128)} fusion(bf16[1536,2880]{1,0:T(8,128)(2,1)} %reshape.107, bf16[1,2880,768]{2,1,0:T(8,128)(2,1)} %param.22), kind=kOutput, calls=%fused_computation.18 | convolution fusion | flops 6794772480 | bytes 17989632 | tf_op jit(solution)/shard_map/dot_general | solution.py:105
  496.1 23.8 %convolution_convert_fusion = bf16[1536,2880]{0,1:T(8,128)(2,1)} fusion(bf16[1,768,2880]{1,2,0:T(8,128)(2,1)} %param.23, f32[1536,768]{1,0:T(8,128)} %fusion.8, bf16[1536,2880]{1,0:T(8,128)(2,1)} %reshape.107, bf16[1,2880,768]{2,1,0:T(8,128)(2,1)} %param.21), kind=kOutput, calls=%fused_computation.11 | convolution fusion | flops 13603405824 | bytes 31260672 | tf_op jit(solution)/shard_map/dot_general | solution.py:110
  520.0 12.5 %copy.81 = bf16[1536,2880]{1,0:T(8,128)(2,1)} copy(bf16[1536,2880]{0,1:T(8,128)(2,1)} %convolution_convert_fusion) | data formatting | bytes 17694720 | tf_op jit(solution)/shard_map/convert_element_type | solution.py:111
  532.4 13.5 %reshape.108 = bf16[128,12,2880]{2,1,0:T(8,128)(2,1)} reshape(bf16[1536,2880]{1,0:T(8,128)(2,1)} %copy.81) | data formatting | bytes 17694720 | tf_op jit(solution)/shard_map/reshape | solution.py:112
  545.9 14.7 %all-to-all-start.2 = ((bf16[128,12,2880]{2,1,0:T(8,128)(2,1)}), bf16[128,12,2880]{2,1,0:T(8,128)(2,1)}, u32[]{:S(2)}, u32[]{:S(2)}) async-start(bf16[128,12,2880]{2,1,0:T(8,128)(2,1)} %reshape.108), calls=%async_computation.2 | async-start | bytes 24117248 | tf_op jit(solution)/shard_map/all_to_all | solution.py:109
  561.2 171.4 %all-to-all-done.2 = bf16[128,12,2880]{2,1,0:T(8,128)(2,1)} async-done(((bf16[128,12,2880]{2,1,0:T(8,128)(2,1)}), bf16[128,12,2880]{2,1,0:T(8,128)(2,1)}, u32[]{:S(2)}, u32[]{:S(2)}) %all-to-all-start.2) | async-done | bytes 8847392 | tf_op jit(solution)/shard_map/all_to_all | solution.py:109
  732.6 8.5 %fusion.6 = bf16[64,12,2880]{2,1,0:T(8,128)(2,1)} fusion(bf16[64,2,12,2880]{3,2,1,0:T(8,128)(2,1)} %bitcast.24), kind=kLoop, calls=%fused_computation.12 | loop fusion | flops 8847360 | bytes 13271040 | tf_op jit(solution)/shard_map/convert_element_type | solution.py:18
  741.1 7.9 %reshape.110 = bf16[768,2880]{1,0:T(8,128)(2,1)} reshape(bf16[64,12,2880]{2,1,0:T(8,128)(2,1)} %fusion.6) | data formatting | bytes 8847360 | tf_op jit(solution)/shard_map/reshape | solution.py:122
  749.0 9.6 %gather_fusion.1 = bf16[512,2880]{1,0:T(8,128)(2,1)} fusion(bf16[768,2880]{1,0:T(8,128)(2,1)} %reshape.110, s32[1024]{0:T(1024)S(1)} %pad_clamp_fusion), kind=kCustom, calls=%fused_computation.1 | custom fusion | bytes 5900288 | tf_op jit(solution)/shard_map/gather | solution.py:123
  758.7 5.9 reshape.111
  (70 shorter events, 47.1 us)
Async XLA Ops:
  6.5 190.4 %copy-start = (bf16[512,2880]{0,1:T(8,128)(2,1)S(1)}, bf16[512,2880]{0,1:T(8,128)(2,1)}, u32[]{:S(2)}) copy-start(bf16[512,2880]{0,1:T(8,128)(2,1)} %param.17) | copy-start | bytes 8847364
  6.5 51.3 %all-gather.3.cloned.1.call-start = ((), (), s32[]{:S(2)}) async-start(), calls=%async_computation.4 | async-start | bytes 1179648 | tf_op jit(solution)/shard_map/all_gather | solution.py:43
  7.3 98.2 %all-gather.5.cloned.1.call-start = ((), (), s32[]{:S(2)}) async-start(), calls=%async_computation.5 | async-start | bytes 1179648 | tf_op jit(solution)/shard_map/all_gather | solution.py:44
  8.0 298.3 %reduce-scatter.4.cloned.1.call-start = ((), (), s32[]{:S(2)}) async-start(), calls=%async_computation.6 | async-start | bytes 6782976 | tf_op jit(solution)/shard_map/reduce_scatter | solution.py:67
  211.8 0.7 copy-start.6
  211.8 1.1 copy-start.4
  211.8 1.5 copy-start.7
  307.6 0.9 copy-start.2
  545.9 14.7 %copy-start.5 = (bf16[2880,64]{0,1:T(8,128)(2,1)S(1)}, bf16[2880,64]{0,1:T(8,128)(2,1)}, u32[]{:S(2)}) copy-start(bf16[2880,64]{0,1:T(8,128)(2,1)} %param.19) | copy-start | bytes 1105924
  545.9 186.8 %all-to-all-start.2 = ((bf16[128,12,2880]{2,1,0:T(8,128)(2,1)}), bf16[128,12,2880]{2,1,0:T(8,128)(2,1)}, u32[]{:S(2)}, u32[]{:S(2)}) async-start(bf16[128,12,2880]{2,1,0:T(8,128)(2,1)} %reshape.108), calls=%async_computation.2 | async-start | bytes 24117248 | tf_op jit(solution)/shard_map/all_to_all | solution.py:109
  758.7 12.9 %copy-start.1 = (bf16[512,2880]{0,1:T(8,128)(2,1)S(1)}, bf16[512,2880]{0,1:T(8,128)(2,1)}, u32[]{:S(2)}) copy-start(bf16[512,2880]{0,1:T(8,128)(2,1)} %param.17) | copy-start | bytes 8847364
  764.6 3.7 copy-start.3
Sparse Core Ops, SparseCore 0:
  9.7 48.1 all-gather.2
  60.2 45.1 all-gather.4
  211.9 94.3 reduce-scatter.3
where the time goes:
time: 787 us; the launch traced here: 779 us
  waiting for transfers between devices  324 us (41%)
  blocking collectives  163 us (21%)
  local copies, waits for them, and re-layouts  134 us (17%)
  matrix products  76 us (10%)
  other arithmetic  52.3 us (7%)
  starting transfers between devices  14.8 us (2%)
  between operations  14.5 us (2%)
    all_to_all x1, waiting for transfers between devices, local(): lax.all_to_all(jnp.dot(active, down_weight[0], preferred_element_type=jnp...  171 us
    all_to_all x1, blocking collectives, local(): lax.all_to_all(doubled, ('seq', 'doc'), split_axis=0, concat_axis=0, tile...  143 us
    reduce_scatter x1, waiting for transfers between devices, local(): lax.psum_scatter(jnp.dot(attended, out_weight, preferred_element_type=jnp...  88.7 us
    all_gather x1, waiting for transfers between devices, local(): piece_keys = lax.all_gather(key_heads, 'seq', axis=1, tiled=True)  46.7 us
    unnamed x1, other arithmetic  24.4 us
    unnamed x24, local copies, waits for them, and re-layouts  23.8 us
    dot_general x1, matrix products, local(): jnp.dot(active, down_weight[0], preferred_element_type=jnp.float32)  23.8 us
    all_to_all x1, blocking collectives, local(): lax.all_to_all(own_out, 'seq', split_axis=2, concat_axis=1, tiled=True)[0]  19.6 us
  transfers between devices with their start and end apart: 4, of which 4 were waited for; matrix products, arithmetic and copies ran while one was open for 5% of the time, Pallas kernels for 0%

commit v1 on v0

v1 whole, which is shorter than its diff:
```python
import functools
import jax
import jax.numpy as jnp
from jax import lax
from jax.experimental import pallas as pl
from jax.experimental.pallas import tpu as pltpu
from jax.sharding import Mesh, PartitionSpec as P

HEADS = 64
KVH = 8
HD = 64
TOP = 4
CAP = 12
EXPERTS = 64
TOK = 128
D = 2880
FF = 768
GW = 512
HALF = 1440
WIDE = 1536
SECOND = D - WIDE
SKIP = HALF - SECOND
PAIR_ROWS = 2 * CAP
ROWS = EXPERTS * PAIR_ROWS

negative_fill = -1e30
swiglu_alpha = 1.702
norm_eps = 1e-05
exp_scale = HD ** (-0.5) * 1.4426950408889634

f32 = jnp.float32
bf16 = jnp.bfloat16
VMEM_SPEC = pl.BlockSpec(memory_space=pltpu.VMEM)
SMEM_SPEC = pl.BlockSpec(memory_space=pltpu.SMEM)
NT = (((1,), (1,)), ((), ()))
TN = (((0,), (0,)), ((), ()))


def attention_kernel(info, qkv, own_w, first_w, second_w, out, keys, vals, att):
    upper = info[0]
    core = info[1]
    doc_len = info[2]
    lane = lax.broadcasted_iota(jnp.int32, (512, 128), 1)
    low = lane < 64
    one = jnp.ones((512, 128), f32)
    for side in range(2):
        base = 1280 - 256 * side
        rows = pl.ds(512 * side, 512)
        kk = qkv[:, base : base + 128].astype(f32)
        vv = qkv[:, base + 128 : base + 256].astype(f32)
        kr = pltpu.roll(kk, 64, 1)
        vr = pltpu.roll(vv, 64, 1)
        for a in range(2):
            for par in range(2):
                keep = low if par == 0 else ~low
                k_src = kk if a == par else kr
                v_src = vv if a == par else vr
                slot = 2 * a + par
                keys[slot, rows, :] = jnp.where(keep, k_src, 0.0).astype(bf16)
                vals[slot, rows, 0:128] = jnp.where(keep, v_src, 0.0).astype(bf16)
                vals[slot, rows, 128:256] = jnp.where(keep, one, 0.0).astype(bf16)

    row_id = lax.broadcasted_iota(jnp.int32, (128, 128), 0)
    col_id = lax.broadcasted_iota(jnp.int32, (128, 128), 1)

    def block(a, pair, i, with_other):
        nk = (i + 1) * 128 + (512 if with_other else 0)
        start = 0 if with_other else 512
        q_rows = slice(i * 128, (i + 1) * 128)
        q_base = pl.multiple_of(a * 512 + pair * 256, 256)
        q_tiles = [
            qkv[q_rows, pl.ds(pl.multiple_of(q_base + 128 * t, 128), 128)] for t in range(2)
        ]
        q_stack = jnp.concatenate(q_tiles, axis=0)
        position = lax.broadcasted_iota(jnp.int32, (1, nk), 1)
        length_bias = jnp.where(position < doc_len, 0.0, negative_fill)
        query = row_id + (nk - 128)
        diag = jnp.where(col_id <= row_id, 0.0, negative_fill) + length_bias[:, nk - 128 :]
        diag = jnp.concatenate([diag] * 2, axis=0)
        total = None
        for par in range(2):
            k_blk = keys[2 * a + par, start : start + nk, :]
            scores = lax.dot_general(q_stack, k_blk, NT, preferred_element_type=f32)
            last = scores[:, nk - 128 :] + diag
            if nk > 128:
                scores = jnp.concatenate(
                    [scores[:, : nk - 128] + length_bias[:, : nk - 128], last], axis=1
                )
            else:
                scores = last
            top = jnp.max(scores, axis=1, keepdims=True)
            weights = jnp.exp2((scores - top) * exp_scale).astype(bf16)
            part = jnp.dot(
                weights, vals[2 * a + par, start : start + nk, :], preferred_element_type=f32
            )
            total = part if total is None else total + part
        result = (total[:, 0:128] / total[:, 128:256]).astype(bf16)
        for t in range(2):
            att[q_rows, pl.ds(pl.multiple_of(q_base + 128 * t, 128), 128)] = result[
                128 * t : 128 * (t + 1)
            ]

    def all_blocks(with_other):
        def body(n, carry):
            for i in range(4):
                block(n // 2, n % 2, i, with_other)
            return carry

        lax.fori_loop(0, 4, body, 0)

    pl.when(upper == 1)(lambda: all_blocks(True))
    pl.when(upper == 0)(lambda: all_blocks(False))

    own = att[:, pl.ds(pl.multiple_of(upper * 512, 512), 512)]
    other = (1 - upper) * 512
    first = att[:, pl.ds(pl.multiple_of(other + core * 256, 256), 256)]
    second = att[:, pl.ds(pl.multiple_of(other + (1 - core) * 256, 256), 256)]
    for lo in range(0, D, 512):
        hi = min(lo + 512, D)
        term = jnp.dot(own, own_w[:, lo:hi], preferred_element_type=f32)
        term += jnp.dot(first, first_w[:, lo:hi], preferred_element_type=f32)
        term += jnp.dot(second, second_w[:, lo:hi], preferred_element_type=f32)
        out[:, lo:hi] = term.astype(bf16)


def norm_kernel(info, parts, hidden, gain, router, ids, residual_out, own_out, send_out, share_out):
    core = info[1]
    acc = hidden[...].astype(f32)
    for z in range(4):
        acc = acc + parts[z].astype(f32)
    rounded = acc.astype(bf16)
    residual_out[...] = rounded
    res = rounded.astype(f32)
    mean_square = jnp.sum(res * res, axis=1, keepdims=True) * (1.0 / D)
    scaled = res * lax.rsqrt(mean_square + norm_eps) * gain[...].astype(f32)
    normed = scaled.astype(bf16)
    logits = lax.dot_general(router[...], normed, NT, preferred_element_type=f32)
    expert = lax.broadcasted_iota(jnp.int32, (EXPERTS, TOK), 0)
    named = expert == ids[0:1, :]
    for k in range(1, TOP):
        named = named | (expert == ids[k : k + 1, :])
    raised = jnp.where(named, jnp.exp(logits), 0.0)
    share_out[...] = raised / jnp.sum(raised, axis=0, keepdims=True)
    lane = lax.broadcasted_iota(jnp.int32, (TOK, WIDE), 1)
    half0 = jnp.where(lane < HALF, scaled[:, :WIDE], 0.0)
    half1 = jnp.where(lane >= SKIP, scaled[:, SECOND:], 0.0)
    own_out[...] = jnp.where(core == 0, half0, half1).astype(bf16)
    send_out[...] = jnp.where(core == 0, half1, half0).astype(bf16)


def slots_of(ids, offset):
    expert = lax.broadcasted_iota(jnp.int32, (EXPERTS, TOK), 0)
    named = expert == ids[0:1, :]
    for k in range(1, TOP):
        named = named | (expert == ids[k : k + 1, :])
    before = lax.broadcasted_iota(jnp.int32, (TOK, TOK), 0) < lax.broadcasted_iota(
        jnp.int32, (TOK, TOK), 1
    )
    rank = jnp.dot(
        named.astype(f32).astype(bf16), before.astype(f32).astype(bf16), preferred_element_type=f32
    )
    return jnp.where(named, rank + offset, -1.0)


def slot_scratch(core, own_ids, other_ids, slots):
    start = (core * CAP).astype(f32)
    slots[:, 0:TOK] = slots_of(own_ids, start)
    slots[:, TOK : 2 * TOK] = slots_of(other_ids, CAP - start)


def hits(slots, first, count):
    block = slots[pl.ds(first, count), :]
    place = lax.broadcasted_iota(jnp.int32, (count, PAIR_ROWS, 2 * TOK), 1).astype(f32)
    return block[:, None, :] == place


EXPERT_BLOCK = 16
ROW_BLOCK = EXPERT_BLOCK * PAIR_ROWS


def dispatch_kernel(info, own, other, own_ids, other_ids, out, slots):
    slot_scratch(info[1], own_ids, other_ids, slots)
    tokens = jnp.concatenate([own[...], other[...]], axis=0)

    def body(n, carry):
        hit = hits(slots, pl.multiple_of(n * EXPERT_BLOCK, EXPERT_BLOCK), EXPERT_BLOCK)
        pick = jnp.where(hit, 1.0, 0.0).reshape(ROW_BLOCK, 2 * TOK).astype(bf16)
        out[pl.ds(pl.multiple_of(n * ROW_BLOCK, ROW_BLOCK), ROW_BLOCK), :] = jnp.dot(
            pick, tokens, preferred_element_type=f32
        ).astype(bf16)
        return carry

    lax.fori_loop(0, EXPERTS // EXPERT_BLOCK, body, 0)


def combine_kernel(info, rows, own_ids, other_ids, own_share, other_share, own_out, other_out, slots, share):
    slot_scratch(info[1], own_ids, other_ids, slots)
    share[:, 0:TOK] = own_share[...]
    share[:, TOK : 2 * TOK] = other_share[...]
    own_out[...] = jnp.zeros_like(own_out)
    other_out[...] = jnp.zeros_like(other_out)

    def body(n, carry):
        first = pl.multiple_of(n * EXPERT_BLOCK, EXPERT_BLOCK)
        hit = hits(slots, first, EXPERT_BLOCK)
        factor = share[pl.ds(first, EXPERT_BLOCK), :][:, None, :]
        factor = jnp.where(hit, factor, 0.0).reshape(ROW_BLOCK, 2 * TOK)
        high = factor.astype(bf16)
        rest = (factor - high.astype(f32)).astype(bf16)
        block = rows[pl.ds(pl.multiple_of(n * ROW_BLOCK, ROW_BLOCK), ROW_BLOCK), :]
        mix = lax.dot_general(high, block, TN, preferred_element_type=f32)
        mix += lax.dot_general(rest, block, TN, preferred_element_type=f32)
        own_out[...] += mix[:TOK]
        other_out[...] += mix[TOK:]
        return carry

    lax.fori_loop(0, EXPERTS // EXPERT_BLOCK, body, 0)


def expert_kernel(info, own, other, gate_w, up_w, down_w, keep_out, send_out, down):
    core = info[1]

    @pl.when(pl.program_id(0) == 0)
    def _():
        down[0] = down_w[:, 0:WIDE]
        down[1] = down_w[:, SECOND:D]

    own_rows = pl.ds(pl.multiple_of(core * SECOND, 64), WIDE)
    other_rows = pl.ds(pl.multiple_of((1 - core) * SECOND, 64), WIDE)
    x_own = own[...]
    x_other = other[...]
    gate = jnp.dot(x_own, gate_w[own_rows, :], preferred_element_type=f32)
    gate += jnp.dot(x_other, gate_w[other_rows, :], preferred_element_type=f32)
    up = jnp.dot(x_own, up_w[own_rows, :], preferred_element_type=f32)
    up += jnp.dot(x_other, up_w[other_rows, :], preferred_element_type=f32)
    active = (gate * jax.nn.sigmoid(swiglu_alpha * gate) * (up + 1.0)).astype(bf16)
    keep_out[...] = jnp.dot(active, down[core], preferred_element_type=f32).astype(bf16)
    send_out[...] = jnp.dot(active, down[1 - core], preferred_element_type=f32).astype(bf16)


def params(mib):
    return pltpu.CompilerParams(vmem_limit_bytes=mib << 20)


def final_kernel(info, residual, own, other, out):
    core = info[1]
    first = jnp.where(core == 0, own[...], other[...])
    second = jnp.where(core == 0, other[...], own[...])
    lane = lax.broadcasted_iota(jnp.int32, (TOK, D), 1)
    blank = jnp.zeros((TOK, SECOND), f32)
    low = jnp.concatenate([first, blank], axis=1)
    high = jnp.concatenate([blank, second], axis=1)
    mix = jnp.where(lane < HALF, low, high)
    out[...] = (residual[...].astype(f32) + mix).astype(bf16)


def local(
    hidden_in,
    queries,
    key_heads,
    values,
    doc_lengths,
    out_weight,
    norm_gain,
    router_weight,
    expert_ids,
    gate_weight,
    up_weight,
    down_weight,
):
    upper = lax.axis_index("xh")
    core = lax.axis_index("c")
    info = jnp.stack([upper, core, doc_lengths[0]]).astype(jnp.int32)
    swap = [(0, 1), (1, 0)]

    half_rows = lax.dynamic_slice_in_dim(out_weight, core * 256, 256, axis=0)
    first_w = lax.ppermute(half_rows, ("xh", "xl"), [(0, 3), (3, 0), (1, 2), (2, 1)])
    second_w = lax.ppermute(first_w, "c", swap)

    ids = expert_ids[0].T
    other_ids = lax.ppermute(ids, "c", swap)

    kv = jnp.concatenate(
        [
            key_heads[0].reshape(TOK, 2, 4, HD).transpose(2, 0, 1, 3).reshape(4, TOK, 128),
            values[0].reshape(TOK, 2, 4, HD).transpose(2, 0, 1, 3).reshape(4, TOK, 128),
        ],
        axis=2,
    )
    lower_kv = lax.ppermute(kv, "xh", [(0, 1)])
    q = queries[0].reshape(TOK, 2, 4, 512).transpose(2, 0, 1, 3).reshape(4, TOK, 1024)
    qkv = lax.all_to_all(
        jnp.concatenate([q, kv, lower_kv], axis=2), "z", split_axis=0, concat_axis=0, tiled=True
    ).reshape(512, 1536)

    partial = pl.pallas_call(
        attention_kernel,
        out_shape=jax.ShapeDtypeStruct((512, D), bf16),
        in_specs=[SMEM_SPEC] + [VMEM_SPEC] * 4,
        out_specs=VMEM_SPEC,
        scratch_shapes=[
            pltpu.VMEM((4, 1024, 128), bf16),
            pltpu.VMEM((4, 1024, 256), bf16),
            pltpu.VMEM((512, 1024), bf16),
        ],
        compiler_params=params(48),
    )(info, qkv, out_weight, first_w, second_w)
    parts = lax.all_to_all(
        partial.reshape(4, TOK, D), "z", split_axis=0, concat_axis=0, tiled=True
    )

    residual, own_half, send_half, share = pl.pallas_call(
        norm_kernel,
        out_shape=[
            jax.ShapeDtypeStruct((TOK, D), bf16),
            jax.ShapeDtypeStruct((TOK, WIDE), bf16),
            jax.ShapeDtypeStruct((TOK, WIDE), bf16),
            jax.ShapeDtypeStruct((EXPERTS, TOK), f32),
        ],
        in_specs=[SMEM_SPEC] + [VMEM_SPEC] * 5,
        out_specs=[VMEM_SPEC] * 4,
        compiler_params=params(40),
    )(info, parts, hidden_in[0], norm_gain[None], router_weight.T, ids)
    other_half = lax.ppermute(send_half, "c", swap)
    other_share = lax.ppermute(share, "c", swap)

    outgoing = pl.pallas_call(
        dispatch_kernel,
        out_shape=jax.ShapeDtypeStruct((ROWS, WIDE), bf16),
        in_specs=[SMEM_SPEC] + [VMEM_SPEC] * 4,
        out_specs=VMEM_SPEC,
        scratch_shapes=[pltpu.VMEM((EXPERTS, 2 * TOK), f32)],
        compiler_params=params(40),
    )(info, own_half, other_half, ids, other_ids)
    chips = ("xh", "z", "xl", "y")
    arrived = lax.all_to_all(
        outgoing.reshape(EXPERTS, PAIR_ROWS, WIDE), chips, split_axis=0, concat_axis=0, tiled=True
    ).reshape(ROWS, WIDE)
    arrived_other = lax.ppermute(arrived, "c", swap)

    step = 256
    keep, send = pl.pallas_call(
        expert_kernel,
        grid=(ROWS // step,),
        out_shape=[jax.ShapeDtypeStruct((ROWS, WIDE), bf16)] * 2,
        in_specs=[
            SMEM_SPEC,
            pl.BlockSpec((step, WIDE), lambda i: (i, 0)),
            pl.BlockSpec((step, WIDE), lambda i: (i, 0)),
            VMEM_SPEC,
            VMEM_SPEC,
            VMEM_SPEC,
        ],
        out_specs=[pl.BlockSpec((step, WIDE), lambda i: (i, 0))] * 2,
        scratch_shapes=[pltpu.VMEM((2, FF, WIDE), bf16)],
        compiler_params=params(52),
    )(info, arrived, arrived_other, gate_weight[0], up_weight[0], down_weight[0])
    sent = lax.ppermute(send, "c", swap)
    expert_out = (keep.astype(f32) + sent.astype(f32)).astype(bf16)

    returned = lax.all_to_all(
        expert_out.reshape(EXPERTS, PAIR_ROWS, WIDE), chips, split_axis=0, concat_axis=0, tiled=True
    ).reshape(ROWS, WIDE)
    own_mix, send_mix = pl.pallas_call(
        combine_kernel,
        out_shape=[jax.ShapeDtypeStruct((TOK, WIDE), f32)] * 2,
        in_specs=[SMEM_SPEC] + [VMEM_SPEC] * 5,
        out_specs=[VMEM_SPEC] * 2,
        scratch_shapes=[pltpu.VMEM((EXPERTS, 2 * TOK), f32)] * 2,
        compiler_params=params(40),
    )(info, returned, ids, other_ids, share, other_share)
    other_mix = lax.ppermute(send_mix, "c", swap)
    layer_out = pl.pallas_call(
        final_kernel,
        out_shape=jax.ShapeDtypeStruct((TOK, D), bf16),
        in_specs=[SMEM_SPEC] + [VMEM_SPEC] * 3,
        out_specs=VMEM_SPEC,
        compiler_params=params(40),
    )(info, residual, own_mix, other_mix)
    return layer_out[None]


def solution(mesh):
    split_mesh = Mesh(mesh.devices.reshape(2, 4, 2, 4, 2), ("xh", "z", "xl", "y", "c"))
    seq = ("xh", "z")
    doc = ("xl", "y", "c")
    in_specs = (
        P(doc, seq, None),
        P(doc, seq, None),
        P(doc, seq, None),
        P(doc, seq, None),
        P(doc),
        P(seq, None),
        P(),
        P(),
        P(doc, seq, None),
        P(seq + doc, None, None),
        P(seq + doc, None, None),
        P(seq + doc, None, None),
    )
    return jax.shard_map(
        local,
        mesh=split_mesh,
        in_specs=in_specs,
        out_specs=P(doc, seq, None),
        check_vma=False,
    )
```

time: 787 us -> 362 us (0.46)
  waiting for transfers between devices: 324 us -> 153 us
  local copies, waits for them, and re-layouts: 134 us -> 34.6 us
  blocking collectives: 163 us -> 76.6 us
  matrix products: 76 us -> 0 us
  Pallas kernels: 0 us -> 56.3 us
  other arithmetic: 52.3 us -> 7.91 us
  between operations: 14.5 us -> 0.89 us
  starting transfers between devices: 14.8 us -> 26.5 us
    reduce_scatter x1 -> x0, waiting for transfers between devices: 88.7 us -> none  [local(): lax.psum_scatter(jnp.dot(attended, out_weight, preferred_element_type=jnp...]
    all_to_all x2 -> x1, blocking collectives: 163 us -> 76.6 us  [local(): lax.all_to_all(outgoing.reshape(EXPERTS, PAIR_ROWS, WIDE), chips, split_a...]
    dot_general x7 -> x0, matrix products: 76 us -> none  [the longest x1 23.8 us: local(): jnp.dot(active, down_weight[0], preferred_element_type=jnp.float32)]
    all_to_all x1 -> x3, waiting for transfers between devices: 171 us -> 106 us  [the longest x1 63 us: local(): lax.all_to_all(expert_out.reshape(EXPERTS, PAIR_ROWS, WIDE), chips, split...]
    all_gather x2 -> x0, waiting for transfers between devices: 62.4 us -> none  [the longest x1 46.7 us: local(): piece_keys = lax.all_gather(key_heads, 'seq', axis=1, tiled=True)]
    pallas_call x0 -> x6, Pallas kernels: none -> 56.3 us  [the longest x1 30.2 us: local(): pl.pallas_call(expert_kernel, grid=(ROWS // step,), out_shape=[jax.ShapeD...]
    reshape x5 -> x4, local copies, waits for them, and re-layouts: 59.1 us -> 5.62 us  [the longest x1 4.59 us: local(): partial.reshape(4, TOK, D)]
    ppermute x0 -> x9, waiting for transfers between devices: none -> 46.9 us  [the longest x1 32.5 us: local(): lax.ppermute(half_rows, ('xh', 'xl'), [(0, 3), (3, 0), (1, 2), (2, 1)])]
  transfers between devices with their start and end apart: 4 -> 12, of which waited for: 4 -> 9; matrix products, arithmetic and copies ran while one was open for 5% -> 6% of each run, Pallas kernels for 0% -> 0%
where the time goes in v1:
time: 362 us; the launch traced here: 356 us
  waiting for transfers between devices  153 us (42%)
  blocking collectives  76.6 us (21%)
  Pallas kernels  56.3 us (16%)
  local copies, waits for them, and re-layouts  34.6 us (10%)
  starting transfers between devices  26.5 us (7%)
  other arithmetic  7.91 us (2%)
    all_to_all x1, blocking collectives, local(): lax.all_to_all(outgoing.reshape(EXPERTS, PAIR_ROWS, WIDE), chips, split_a...  76.6 us
    all_to_all x1, waiting for transfers between devices, local(): lax.all_to_all(expert_out.reshape(EXPERTS, PAIR_ROWS, WIDE), chips, split...  63 us
    all_to_all x1, waiting for transfers between devices, local(): lax.all_to_all(partial.reshape(4, TOK, D), 'z', split_axis=0, concat_axis...  32.8 us
    ppermute x1, waiting for transfers between devices, local(): lax.ppermute(half_rows, ('xh', 'xl'), [(0, 3), (3, 0), (1, 2), (2, 1)])  32.5 us
    pallas_call x1, Pallas kernels, local(): pl.pallas_call(expert_kernel, grid=(ROWS // step,), out_shape=[jax.ShapeD...  30.2 us
    unnamed x25, local copies, waits for them, and re-layouts  16.8 us
    pallas_call x1, Pallas kernels, local(): pl.pallas_call(attention_kernel, out_shape=jax.ShapeDtypeStruct((512, D),...  14.2 us
    all_to_all x1, waiting for transfers between devices, local(): lax.all_to_all(jnp.concatenate([q, kv, lower_kv], axis=2), 'z', split_axi...  10.2 us
  transfers between devices with their start and end apart: 12, of which 9 were waited for; matrix products, arithmetic and copies ran while one was open for 6% of the time, Pallas kernels for 0%

profile of v1, /device:TPU:32, one launch (start us, length us, event | category | flops | bytes accessed | tf_op | source)
XLA Modules:
  0.0 355.8 jit_solution(1521674568695361574)
XLA Ops:
  1.6 2.8 collective-permute-start.1
  6.3 2.7 collective-permute-start
  9.0 32.5 %collective-permute-done.1 = bf16[256,2880]{0,1:T(8,128)(2,1)} collective-permute-done((bf16[256,2880]{0,1:T(8,128)(2,1)S(1)}, bf16[256,2880]{0,1:T(8,128)(2,1)}, u32[]{:S(2)}, u32[]{:S(2)}) %collective-permute-start.1) | collective-permute-done | bytes 1474592 | tf_op jit(solution)/shard_map/ppermute | solution.py:277
  45.7 5.4 %all-to-all-start = ((bf16[4,128,1536]{2,1,0:T(8,128)(2,1)}), bf16[4,128,1536]{2,1,0:T(8,128)(2,1)S(1)}, u32[]{:S(2)}, u32[]{:S(2)}) async-start(bf16[4,128,1536]{2,1,0:T(8,128)(2,1)} %pad_maximum_fusion), calls=%async_computation | async-start | bytes 3145728 | tf_op jit(solution)/shard_map/all_to_all | solution.py:292
  51.1 4.6 %copy.42.own_w = bf16[512,2880]{1,0:T(8,128)(2,1)} copy(bf16[512,2880]{0,1:T(8,128)(2,1)} %param.17) | data formatting | bytes 5898240 | tf_op args[5]
  56.4 1.8 copy.43.first_w
  58.3 2.6 copy.44.second_w
  60.8 10.2 %all-to-all-done = bf16[4,128,1536]{2,1,0:T(8,128)(2,1)S(1)} async-done(((bf16[4,128,1536]{2,1,0:T(8,128)(2,1)}), bf16[4,128,1536]{2,1,0:T(8,128)(2,1)S(1)}, u32[]{:S(2)}, u32[]{:S(2)}) %all-to-all-start) | async-done | bytes 1572896 | tf_op jit(solution)/shard_map/all_to_all | solution.py:292
  72.4 14.2 %shard_map.118 = bf16[512,2880]{1,0:T(8,128)(2,1)} custom-call(s32[3]{0:T(128)S(1)} %pad_add_fusion.info, bf16[512,1536]{1,0:T(8,128)(2,1)S(1)} %bitcast.27, bf16[512,2880]{1,0:T(8,128)(2,1)} %copy.42.own_w, bf16[256,2880]{1,0:T(8,128)(2,1)S(1)} %copy.43.first_w, bf16[256,2880]{1,0:T(8,128)(2,1)S(1)} %copy-done), custom_call_target="tpu_custom_call" | custom-call | tf_op jit(solution)/shard_map/pallas_call | solution.py:296
  86.7 4.6 %copy.45 = bf16[4,128,2880]{1,2,0:T(8,128)(2,1)} copy(bf16[4,128,2880]{2,1,0:T(8,128)(2,1)} %bitcast.37) | data formatting | bytes 5898240 | tf_op jit(solution)/shard_map/reshape | solution.py:309
  91.3 6.2 %all-to-all-start.1 = ((bf16[4,128,2880]{1,2,0:T(8,128)(2,1)}), bf16[4,128,2880]{1,2,0:T(8,128)(2,1)}, u32[]{:S(2)}, u32[]{:S(2)}) async-start(bf16[4,128,2880]{1,2,0:T(8,128)(2,1)} %copy.45), calls=%async_computation.1 | async-start | bytes 5898240 | tf_op jit(solution)/shard_map/all_to_all | solution.py:308
  98.6 32.8 %all-to-all-done.1 = bf16[4,128,2880]{1,2,0:T(8,128)(2,1)} async-done(((bf16[4,128,2880]{1,2,0:T(8,128)(2,1)}), bf16[4,128,2880]{1,2,0:T(8,128)(2,1)}, u32[]{:S(2)}, u32[]{:S(2)}) %all-to-all-start.1) | async-done | bytes 2949152 | tf_op jit(solution)/shard_map/all_to_all | solution.py:308
  131.4 3.3 copy.47.parts
  140.2 2.6 shard_map.120
  142.8 76.6 %all_to_all.20 = bf16[64,24,1536]{2,1,0:T(8,128)(2,1)} all-to-all(bf16[64,24,1536]{2,1,0:T(8,128)(2,1)S(1)} %bitcast.26), channel_id=1, replica_groups=mesh['xh'=2,'z'=4,'xl'=2,'y'=4,'c'=2] {'xh','z','xl','y'}, dimensions={0} | all-to-all | bytes 9437184 | tf_op jit(solution)/shard_map/all_to_all | solution.py:336
  219.5 6.5 %copy.48 = bf16[1,768,2880]{2,1,0:T(8,128)(2,1)} copy(bf16[1,768,2880]{1,2,0:T(8,128)(2,1)} %param.23) | data formatting | bytes 8847360 | tf_op args[11]
  226.0 1.7 collective-permute-done.5.other
  227.7 30.2 %shard_map.121 = (bf16[1536,1536]{1,0:T(8,128)(2,1)}, bf16[1536,1536]{1,0:T(8,128)(2,1)}) custom-call(s32[3]{0:T(128)S(1)} %pad_add_fusion.info, bf16[1536,1536]{1,0:T(8,128)(2,1)} %bitcast.17.own, bf16[1536,1536]{1,0:T(8,128)(2,1)} %collective-permute-done.5.other, bf16[2880,768]{1,0:T(8,128)(2,1)} %bitcast.38, bf16[2880,768]{1,0:T(8,128)(2,1)} %bitcast.39, ...), custom_call_target="tpu_custom_call" | custom-call | tf_op jit(solution)/shard_map/pallas_call | solution.py:342
  258.1 8.0 %collective-permute-done.6 = bf16[1536,1536]{1,0:T(8,128)(2,1)S(1)} collective-permute-done((bf16[1536,1536]{1,0:T(8,128)(2,1)}, bf16[1536,1536]{1,0:T(8,128)(2,1)S(1)}, u32[]{:S(2)}, u32[]{:S(2)}) %collective-permute-start.6) | collective-permute-done | bytes 4718624 | tf_op jit(solution)/shard_map/ppermute | solution.py:358
  266.1 5.8 %add_convert_fusion = bf16[1536,1536]{1,0:T(8,128)(2,1)} fusion(bf16[1536,1536]{1,0:T(8,128)(2,1)S(1)} %collective-permute-done.6, bf16[1536,1536]{1,0:T(8,128)(2,1)} %get-tuple-element.16), kind=kLoop, calls=%fused_computation | loop fusion | flops 9437184 | bytes 14155776 | tf_op jit(solution)/shard_map/convert_element_type | solution.py:359
  271.9 8.5 %all-to-all-start.3 = ((bf16[64,24,1536]{2,1,0:T(8,128)(2,1)}), bf16[64,24,1536]{2,1,0:T(8,128)(2,1)}, u32[]{:S(2)}, u32[]{:S(2)}) async-start(bf16[64,24,1536]{2,1,0:T(8,128)(2,1)} %bitcast.35), calls=%async_computation.3 | async-start | bytes 9437184 | tf_op jit(solution)/shard_map/all_to_all | solution.py:361
  281.7 63.0 %all-to-all-done.3 = bf16[64,24,1536]{2,1,0:T(8,128)(2,1)} async-done(((bf16[64,24,1536]{2,1,0:T(8,128)(2,1)}), bf16[64,24,1536]{2,1,0:T(8,128)(2,1)}, u32[]{:S(2)}, u32[]{:S(2)}) %all-to-all-start.3) | async-done | bytes 4718624 | tf_op jit(solution)/shard_map/all_to_all | solution.py:361
  344.8 6.6 %shard_map.122 = (f32[128,1536]{1,0:T(8,128)S(1)}, f32[128,1536]{1,0:T(8,128)S(1)}) custom-call(s32[3]{0:T(128)S(1)} %pad_add_fusion.info, bf16[1536,1536]{1,0:T(8,128)(2,1)} %bitcast.22.rows, s32[4,128]{1,0:T(4,128)S(1)} %bitcast.34, s32[4,128]{1,0:T(4,128)S(1)} %collective-permute-done.4.other_ids, f32[64,128]{1,0:T(8,128)S(1)} %get-tuple-element.18.own_share, ...), custom_call_target="tpu_custom_call" | custom-call | tf_op jit(solution)/shard_map/pallas_call | solution.py:364
  351.5 2.3 collective-permute-done.8.other
  (51 shorter events, 19.1 us)
Async XLA Ops:
  0.0 5.5 %copy-start.8 = (bf16[1,128,512]{2,1,0:T(8,128)(2,1)S(1)}, bf16[1,128,512]{2,1,0:T(8,128)(2,1)}, u32[]{:S(2)}) copy-start(bf16[1,128,512]{2,1,0:T(8,128)(2,1)} %param.15) | copy-start | bytes 393220
  0.0 41.9 %copy-start.6 = (bf16[1,128,4096]{2,1,0:T(8,128)(2,1)S(1)}, bf16[1,128,4096]{2,1,0:T(8,128)(2,1)}, u32[]{:S(2)}) copy-start(bf16[1,128,4096]{2,1,0:T(8,128)(2,1)} %param.13) | copy-start | bytes 3145732
  1.6 40.0 %collective-permute-start.1 = (bf16[256,2880]{0,1:T(8,128)(2,1)S(1)}, bf16[256,2880]{0,1:T(8,128)(2,1)}, u32[]{:S(2)}, u32[]{:S(2)}) collective-permute-start(bf16[256,2880]{0,1:T(8,128)(2,1)S(1)} %constant_dynamic-slice_fusion), channel_id=1, source_target_pairs={{0,72},{72,0},{8,64},{64,8},{1,73},{73,1},{9,65},{65,9},{2,74},{74... | collective-permute-start | bytes 4423688 | tf_op jit(solution)/shard_map/ppermute | solution.py:277
  6.3 37.9 %collective-permute-start = (bf16[4,128,256]{1,2,0:T(8,128)(2,1)}, bf16[4,128,256]{1,2,0:T(8,128)(2,1)S(1)}, u32[]{:S(2)}, u32[]{:S(2)}) collective-permute-start(bf16[4,128,256]{1,2,0:T(8,128)(2,1)} %pad_maximum_fusion.1), channel_id=1, source_target_pairs={{0,64},{1,65},{2,66},{3,67},{4,68},{5,69},{6,70},{7,71},{8,72},{9,... | collective-permute-start | bytes 786440 | tf_op jit(solution)/shard_map/ppermute | solution.py:290
  41.6 16.7 %collective-permute-start.2 = (bf16[256,2880]{0,1:T(8,128)(2,1)}, bf16[256,2880]{0,1:T(8,128)(2,1)}, u32[]{:S(2)}, u32[]{:S(2)}) collective-permute-start(bf16[256,2880]{0,1:T(8,128)(2,1)} %collective-permute-done.1), channel_id=1, source_target_pairs={{0,1},{1,0},{2,3},{3,2},{4,5},{5,4},{6,7},{7,6},{8,9},{9,8},{10,11... | collective-permute-start | bytes 4423688 | tf_op jit(solution)/shard_map/ppermute | solution.py:278
  45.7 25.3 %all-to-all-start = ((bf16[4,128,1536]{2,1,0:T(8,128)(2,1)}), bf16[4,128,1536]{2,1,0:T(8,128)(2,1)S(1)}, u32[]{:S(2)}, u32[]{:S(2)}) async-start(bf16[4,128,1536]{2,1,0:T(8,128)(2,1)} %pad_maximum_fusion), calls=%async_computation | async-start | bytes 3145728 | tf_op jit(solution)/shard_map/all_to_all | solution.py:292
  71.1 1.4 copy-start
  91.3 6.2 %copy-start.7 = (bf16[1,128,2880]{1,2,0:T(8,128)(2,1)S(1)}, bf16[1,128,2880]{1,2,0:T(8,128)(2,1)}, u32[]{:S(2)}) copy-start(bf16[1,128,2880]{1,2,0:T(8,128)(2,1)} %param.12) | copy-start | bytes 2211844
  91.3 7.3 %copy-start.9 = (bf16[2880]{0:T(1024)(128)(2,1)S(1)}, bf16[2880]{0:T(1024)(128)(2,1)}, u32[]{:S(2)}) copy-start(bf16[2880]{0:T(1024)(128)(2,1)} %param.18) | copy-start | bytes 17284
  91.3 40.1 %all-to-all-start.1 = ((bf16[4,128,2880]{1,2,0:T(8,128)(2,1)}), bf16[4,128,2880]{1,2,0:T(8,128)(2,1)}, u32[]{:S(2)}, u32[]{:S(2)}) async-start(bf16[4,128,2880]{1,2,0:T(8,128)(2,1)} %copy.45), calls=%async_computation.1 | async-start | bytes 5898240 | tf_op jit(solution)/shard_map/all_to_all | solution.py:308
  98.6 36.1 %copy-start.4 = (bf16[2880,64]{0,1:T(8,128)(2,1)S(1)}, bf16[2880,64]{0,1:T(8,128)(2,1)}, u32[]{:S(2)}) copy-start(bf16[2880,64]{0,1:T(8,128)(2,1)} %param.19) | copy-start | bytes 1105924
  98.6 36.1 %copy-start.5 = (s32[1,128,4]{1,2,0:T(4,128)S(1)}, s32[1,128,4]{1,2,0:T(4,128)}, u32[]{:S(2)}) copy-start(s32[1,128,4]{1,2,0:T(4,128)} %param.20) | copy-start | bytes 6148
  134.8 1.1 copy-start.1
  137.6 0.9 copy-start.2
  138.5 1.7 collective-permute-start.3
  138.5 1.7 collective-permute-start.4
  219.5 8.3 %collective-permute-start.5 = (bf16[1536,1536]{1,0:T(8,128)(2,1)}, bf16[1536,1536]{1,0:T(8,128)(2,1)}, u32[]{:S(2)}, u32[]{:S(2)}) collective-permute-start(bf16[1536,1536]{1,0:T(8,128)(2,1)} %bitcast.17.own), channel_id=1, source_target_pairs={{0,1},{1,0},{2,3},{3,2},{4,5},{5,4},{6,7},{7,6},{8,9},{9,8},{10,11... | collective-permute-start | bytes 14155784 | tf_op jit(solution)/shard_map/ppermute | solution.py:339
  258.0 8.1 %collective-permute-start.6 = (bf16[1536,1536]{1,0:T(8,128)(2,1)}, bf16[1536,1536]{1,0:T(8,128)(2,1)S(1)}, u32[]{:S(2)}, u32[]{:S(2)}) collective-permute-start(bf16[1536,1536]{1,0:T(8,128)(2,1)} %get-tuple-element.17), channel_id=1, source_target_pairs={{0,1},{1,0},{2,3},{3,2},{4,5},{5,4},{6,7},{7,6},{8,9},{9,8},{10,11... | collective-permute-start | bytes 14155784 | tf_op jit(solution)/shard_map/ppermute | solution.py:358
  271.9 72.9 %all-to-all-start.3 = ((bf16[64,24,1536]{2,1,0:T(8,128)(2,1)}), bf16[64,24,1536]{2,1,0:T(8,128)(2,1)}, u32[]{:S(2)}, u32[]{:S(2)}) async-start(bf16[64,24,1536]{2,1,0:T(8,128)(2,1)} %bitcast.35), calls=%async_computation.3 | async-start | bytes 9437184 | tf_op jit(solution)/shard_map/all_to_all | solution.py:361
  280.5 73.3 %copy-start.3 = (bf16[128,2880]{1,0:T(8,128)(2,1)S(1)}, bf16[128,2880]{1,0:T(8,128)(2,1)}, u32[]{:S(2)}) copy-start(bf16[128,2880]{1,0:T(8,128)(2,1)} %copy-done.2) | copy-start | bytes 2211844
  280.5 1.3 collective-permute-start.7
  351.4 2.4 collective-permute-start.8
